TPU v7x, 32 devices: a whole 2x2x4 slice. The times are simulated.
32 devices in a mesh: dp: 4 (over y, x), expert: 8 (over z, core).
Axes of the slice: x: 2, y: 2, z: 4, core: 2. Of those that a mesh axis runs over, the one named last changes fastest.
Arguments:
- tokens: bfloat16 [4096, 1280], P(('dp', 'expert')), may hold values from -6 to 6
- cotangent: bfloat16 [4096, 1280], P(('dp', 'expert')), may hold values from -6 to 6
- routes: int32 [4096, 6], P(('dp', 'expert')), may hold values from 0 to 14, all different within a row; in each aligned block of 128 rows (0 to 127, 128 to 255, ...) at most 64 rows name the same one
- expert_at: int32 [16], replicated, may hold values from 0 to 15, each once
- norm1_gain: float32 [1280], replicated, may hold values from 0.5 to 1.5
- w_query: bfloat16 [1280, 1280], replicated, may hold values from -0.15625 to 0.15625
- w_key: bfloat16 [1280, 1280], replicated, may hold values from -0.15625 to 0.15625
- w_value: bfloat16 [1280, 1280], replicated, may hold values from -0.15625 to 0.15625
- w_out: bfloat16 [1280, 1280], replicated, may hold values from -1 to 1
- norm2_gain: float32 [1280], replicated, may hold values from 0.5 to 1.5
- w_router: bfloat16 [1280, 15], replicated, may hold values from -0.078125 to 0.078125
- shared_gate: bfloat16 [1280, 896], replicated, may hold values from -0.15625 to 0.15625
- shared_up: bfloat16 [1280, 896], replicated, may hold values from -0.15625 to 0.15625
- shared_down: bfloat16 [896, 1280], replicated, may hold values from -0.1875 to 0.1875
- routed_gate: bfloat16 [16, 1280, 896], P('expert'), may hold values from -0.15625 to 0.15625
- routed_up: bfloat16 [16, 1280, 896], P('expert'), may hold values from -0.15625 to 0.15625
- routed_down: bfloat16 [16, 896, 1280], P('expert'), may hold values from -0.875 to 0.875
Outputs:
- output: bfloat16 [4096, 1280], P(('dp', 'expert'))
- grad_tokens: float32 [4096, 1280], P(('dp', 'expert'))
- grad_norm1: float32 [1280], P(('dp', 'expert'))
- grad_query: float32 [1280, 1280], P(('dp', 'expert'))
- grad_key: float32 [1280, 1280], P(('dp', 'expert'))
- grad_value: float32 [1280, 1280], P(('dp', 'expert'))
- grad_out: float32 [1280, 1280], P(('dp', 'expert'))
- grad_norm2: float32 [1280], P(('dp', 'expert'))
- grad_router: float32 [1280, 15], P(('dp', 'expert'))
- grad_shared_gate: float32 [1280, 896], P(('dp', 'expert'))
- grad_shared_up: float32 [1280, 896], P(('dp', 'expert'))
- grad_shared_down: float32 [896, 1280], P(('dp', 'expert'))
- grad_routed_gate: float32 [16, 1280, 896], P('expert', 'dp')
- grad_routed_up: float32 [16, 1280, 896], P('expert', 'dp')
- grad_routed_down: float32 [16, 896, 1280], P('expert', 'dp')
Inputs may be any that keep to these rules, and one draw needn't show every extreme that they name: `routes`: each token names 6 different experts. Among the 128 tokens of one device no expert is named more than 64 times, a bound that some block reaches. `expert_at`: each slot holds one expert; every value appears once, and the slot holding the value 15 is empty.
All inputs are finite; a program needn't handle non-finite values.
Results may differ from a plain program's by a relative error of at most 0.015.
Values may be sent and summed in bfloat16 or wider, within the bound.
No kernel may reach another device: no remote copies, remote signals or barrier semaphores. Data moves between devices by JAX's collectives and lax.ppermute only.
A program may use at most 320 MiB of HBM per device.

v0:
```python
import math

import jax
import jax.numpy as jnp
from jax import lax
from jax.sharding import PartitionSpec as P

HEADS = 10
HEAD_DIM = 128
TOP = 6


epsilon = 1e-06


def swish_of(operand):
    return operand * jax.nn.sigmoid(operand)


def rotary_tables(length, half_width):
    position = jnp.arange(length, dtype=jnp.float32)[:, None]
    frequencies = jnp.exp(
        jnp.arange(half_width, dtype=jnp.float32) * (-math.log(10000.0) / half_width)
    )
    angles = position * frequencies[None, :]
    return (jnp.cos(angles)[:, None, :], jnp.sin(angles)[:, None, :])


def rotate(operand, cosine, sine_table, direction):
    half_width = operand.shape[-1] // 2
    first_half = operand[..., :half_width]
    second = operand[..., half_width:]
    return jnp.concatenate(
        [
            first_half * cosine - direction * second * sine_table,
            second * cosine + direction * first_half * sine_table,
        ],
        -1,
    )


def product(left, right):
    return jnp.dot(left, right, preferred_element_type=jnp.float32)


def product_left(left, right):
    return lax.dot_general(
        left, right, (((0,), (0,)), ((), ())), preferred_element_type=jnp.float32
    )


def product_right(left, right):
    return lax.dot_general(
        left, right, (((1,), (1,)), ((), ())), preferred_element_type=jnp.float32
    )


def norm_backward(grad_normed, unit_rows, row_scale, gain):
    scaled_grad = grad_normed * gain
    grad_gain = jnp.sum(grad_normed * unit_rows, 0)
    grad_rows = row_scale * (
        scaled_grad - unit_rows * jnp.mean(scaled_grad * unit_rows, -1, keepdims=True)
    )
    return (grad_rows, grad_gain)


def shards(
    tokens,
    cotangent,
    routes,
    expert_at,
    norm1_gain,
    w_query,
    w_key,
    w_value,
    w_out,
    norm2_gain,
    w_router,
    shared_gate,
    shared_up,
    shared_down,
    routed_gate,
    routed_up,
    routed_down,
):
    length, model_width = tokens.shape
    expert_count = w_router.shape[1]
    slot_count = expert_at.shape[0]
    slot_dev = routed_gate.shape[0]
    owners = lax.axis_size("expert")
    capacity = (length * TOP * 5 // (4 * expert_count) + 7) // 8 * 8
    score_scale = 1.0 / math.sqrt(HEAD_DIM)
    inputs_f = tokens.astype(jnp.float32)
    scale_first = lax.rsqrt(jnp.mean(inputs_f * inputs_f, -1, keepdims=True) + epsilon)
    unit_first = inputs_f * scale_first
    normed_first = (unit_first * norm1_gain).astype(jnp.bfloat16)
    cosine, sine_table = rotary_tables(length, HEAD_DIM // 2)

    def heads_of(weight):
        return product(normed_first, weight).reshape(length, HEADS, HEAD_DIM)

    queries = rotate(heads_of(w_query), cosine, sine_table, 1.0).astype(jnp.bfloat16)
    key_heads = rotate(heads_of(w_key), cosine, sine_table, 1.0).astype(jnp.bfloat16)
    value_heads = heads_of(w_value).astype(jnp.bfloat16)
    causal = jnp.arange(length)[:, None] >= jnp.arange(length)[None, :]

    def masked_scores():
        raw_scores = (
            jnp.einsum("qhd,khd->hqk", queries, key_heads, preferred_element_type=jnp.float32)
            * score_scale
        )
        return jnp.where(causal[None], raw_scores, -1e30)

    scores_fwd = masked_scores()
    row_max = jnp.max(scores_fwd, -1, keepdims=True)
    expo_terms = jnp.exp(scores_fwd - row_max)
    row_total = jnp.sum(expo_terms, -1, keepdims=True)
    log_total = row_max + jnp.log(row_total)
    probs_low = (expo_terms / row_total).astype(jnp.bfloat16)
    attended = (
        jnp.einsum("hqk,khd->qhd", probs_low, value_heads, preferred_element_type=jnp.float32)
        .reshape(length, model_width)
        .astype(jnp.bfloat16)
    )
    residual = inputs_f + product(attended, w_out)
    scale_second = lax.rsqrt(jnp.mean(residual * residual, -1, keepdims=True) + epsilon)
    unit_second = residual * scale_second
    normed_second = (unit_second * norm2_gain).astype(jnp.bfloat16)
    shared_g = product(normed_second, shared_gate)
    shared_u = product(normed_second, shared_up)
    shared_hidden = (swish_of(shared_g) * shared_u).astype(jnp.bfloat16)
    shared_result = product(shared_hidden, shared_down)
    logits = product(normed_second, w_router)
    logit_max = jnp.max(logits, -1, keepdims=True)
    logit_terms = jnp.exp(logits - logit_max)
    router_probs = logit_terms / jnp.sum(logit_terms, -1, keepdims=True)
    expert_ids = jnp.arange(expert_count, dtype=jnp.int32)
    chosen = (routes[:, :, None] == expert_ids[None, None, :]).astype(jnp.float32)
    gate_values = jnp.sum(chosen * router_probs[:, None, :], -1)
    flat_ids = routes.reshape(-1)
    onehot = (flat_ids[:, None] == expert_ids[None, :]).astype(jnp.int32)
    position = jnp.sum(jnp.cumsum(onehot, 0) * onehot, 1) - 1
    slot_of = jnp.sum(
        jnp.where(
            expert_at[None, :] == expert_ids[:, None],
            jnp.arange(slot_count, dtype=jnp.int32)[None, :],
            0,
        ),
        1,
    )
    target_row = jnp.sum(onehot * slot_of[None, :], 1) * capacity + position
    token_rows = jnp.broadcast_to(normed_second[:, None, :], (length, TOP, model_width)).reshape(
        length * TOP, model_width
    )
    send_rows = (
        jnp.zeros((slot_count * capacity, model_width), jnp.bfloat16).at[target_row].set(token_rows)
    )
    send_rows = send_rows.reshape(owners, slot_dev, capacity, model_width)
    received = lax.all_to_all(send_rows, "expert", split_axis=0, concat_axis=0, tiled=True)
    expert_g = jnp.einsum(
        "nscd,sdf->nscf", received, routed_gate, preferred_element_type=jnp.float32
    )
    expert_u = jnp.einsum("nscd,sdf->nscf", received, routed_up, preferred_element_type=jnp.float32)
    expert_hidden = (swish_of(expert_g) * expert_u).astype(jnp.bfloat16)
    expert_result = jnp.einsum(
        "nscf,sfd->nscd", expert_hidden, routed_down, preferred_element_type=jnp.float32
    ).astype(jnp.bfloat16)
    expert_result, kept_rows = (expert_result, received)
    returned = lax.all_to_all(expert_result, "expert", split_axis=0, concat_axis=0, tiled=True)
    returned_rows = returned.reshape(slot_count * capacity, model_width)[target_row]
    returned_rows = returned_rows.reshape(length, TOP, model_width).astype(jnp.float32)
    output = (
        residual + shared_result + jnp.sum(gate_values[:, :, None] * returned_rows, 1)
    ).astype(jnp.bfloat16)
    grad_output = cotangent.astype(jnp.float32)
    d_result = (gate_values[:, :, None] * grad_output[:, None, :]).astype(jnp.bfloat16)
    d_gates = jnp.sum(grad_output[:, None, :] * returned_rows, -1)
    send_grads = (
        jnp.zeros((slot_count * capacity, model_width), jnp.bfloat16)
        .at[target_row]
        .set(d_result.reshape(length * TOP, model_width))
        .reshape(owners, slot_dev, capacity, model_width)
    )
    grad_received, expert_inputs = (
        lax.all_to_all(send_grads, "expert", split_axis=0, concat_axis=0, tiled=True),
        lax.all_to_all(send_rows, "expert", split_axis=0, concat_axis=0, tiled=True),
    )
    expert_g = jnp.einsum(
        "nscd,sdf->nscf", expert_inputs, routed_gate, preferred_element_type=jnp.float32
    )
    expert_u = jnp.einsum(
        "nscd,sdf->nscf", expert_inputs, routed_up, preferred_element_type=jnp.float32
    )
    sigmoid_gate = jax.nn.sigmoid(expert_g)
    activated = expert_g * sigmoid_gate
    expert_hidden = (activated * expert_u).astype(jnp.bfloat16)
    d_hidden = jnp.einsum(
        "nscd,sfd->nscf", grad_received, routed_down, preferred_element_type=jnp.float32
    )
    grad_rdown = jnp.einsum(
        "nscf,nscd->sfd", expert_hidden, grad_received, preferred_element_type=jnp.float32
    )
    d_expert_g = (
        d_hidden * expert_u * sigmoid_gate * (1.0 + expert_g * (1.0 - sigmoid_gate))
    ).astype(jnp.bfloat16)
    d_expert_u = (d_hidden * activated).astype(jnp.bfloat16)
    grad_rgate = jnp.einsum(
        "nscd,nscf->sdf", expert_inputs, d_expert_g, preferred_element_type=jnp.float32
    )
    grad_rup = jnp.einsum(
        "nscd,nscf->sdf", expert_inputs, d_expert_u, preferred_element_type=jnp.float32
    )
    d_rows = (
        jnp.einsum("nscf,sdf->nscd", d_expert_g, routed_gate, preferred_element_type=jnp.float32)
        + jnp.einsum("nscf,sdf->nscd", d_expert_u, routed_up, preferred_element_type=jnp.float32)
    ).astype(jnp.bfloat16)
    grad_rgate, grad_rup, grad_rdown = (
        lax.psum_scatter(
            grad_rgate.astype(jnp.bfloat16), "dp", scatter_dimension=1, tiled=True
        ).astype(jnp.float32),
        lax.psum_scatter(
            grad_rup.astype(jnp.bfloat16), "dp", scatter_dimension=1, tiled=True
        ).astype(jnp.float32),
        lax.psum_scatter(
            grad_rdown.astype(jnp.bfloat16), "dp", scatter_dimension=1, tiled=True
        ).astype(jnp.float32),
    )
    rows_back = lax.all_to_all(d_rows, "expert", split_axis=0, concat_axis=0, tiled=True)
    rows_back = rows_back.reshape(slot_count * capacity, model_width)[target_row]
    routed_grad = jnp.sum(rows_back.reshape(length, TOP, model_width).astype(jnp.float32), 1)
    d_probs = jnp.sum(chosen * d_gates[:, :, None], 1)
    d_logits = (
        router_probs * (d_probs - jnp.sum(router_probs * d_probs, -1, keepdims=True))
    ).astype(jnp.bfloat16)
    grad_router = product_left(normed_second, d_logits)
    d_shared = grad_output.astype(jnp.bfloat16)
    grad_sdown = product_left(shared_hidden, d_shared)
    d_shared_hidden = product_right(d_shared, shared_down)
    shared_sigmoid = jax.nn.sigmoid(shared_g)
    shared_act = shared_g * shared_sigmoid
    d_shared_g = (
        d_shared_hidden * shared_u * shared_sigmoid * (1.0 + shared_g * (1.0 - shared_sigmoid))
    ).astype(jnp.bfloat16)
    d_shared_u = (d_shared_hidden * shared_act).astype(jnp.bfloat16)
    grad_sgate = product_left(normed_second, d_shared_g)
    grad_sup = product_left(normed_second, d_shared_u)
    d_normed_second = (
        product_right(d_shared_g, shared_gate)
        + product_right(d_shared_u, shared_up)
        + product_right(d_logits, w_router)
        + routed_grad
    )
    d_second, grad_gain_second = norm_backward(
        d_normed_second, unit_second, scale_second, norm2_gain
    )
    d_residual = grad_output + d_second
    d_branch = d_residual.astype(jnp.bfloat16)
    grad_wout = product_left(attended, d_branch)
    d_attended = (
        product_right(d_branch, w_out).astype(jnp.bfloat16).reshape(length, HEADS, HEAD_DIM)
    )
    att_probs = jnp.exp(masked_scores() - log_total)
    d_att = jnp.einsum("qhd,khd->hqk", d_attended, value_heads, preferred_element_type=jnp.float32)
    d_scores = (att_probs * (d_att - jnp.sum(att_probs * d_att, -1, keepdims=True))).astype(
        jnp.bfloat16
    )
    d_values = (
        jnp.einsum(
            "hqk,qhd->khd",
            att_probs.astype(jnp.bfloat16),
            d_attended,
            preferred_element_type=jnp.float32,
        )
        .astype(jnp.bfloat16)
        .reshape(length, model_width)
    )
    d_query_rot = (
        jnp.einsum("hqk,khd->qhd", d_scores, key_heads, preferred_element_type=jnp.float32)
        * score_scale
    )
    d_key_rot = (
        jnp.einsum("hqk,qhd->khd", d_scores, queries, preferred_element_type=jnp.float32)
        * score_scale
    )
    d_queries = (
        rotate(d_query_rot, cosine, sine_table, -1.0)
        .astype(jnp.bfloat16)
        .reshape(length, model_width)
    )
    d_keys = (
        rotate(d_key_rot, cosine, sine_table, -1.0)
        .astype(jnp.bfloat16)
        .reshape(length, model_width)
    )
    grad_wquery = product_left(normed_first, d_queries)
    grad_wkey = product_left(normed_first, d_keys)
    grad_wvalue = product_left(normed_first, d_values)
    d_normed_first = (
        product_right(d_queries, w_query)
        + product_right(d_keys, w_key)
        + product_right(d_values, w_value)
    )
    d_first, grad_gain_first = norm_backward(d_normed_first, unit_first, scale_first, norm1_gain)
    grad_inputs = d_residual + d_first
    summed = (
        lax.psum_scatter(grad_gain_first, ("dp", "expert"), scatter_dimension=0, tiled=True),
        lax.psum_scatter(grad_wquery, ("dp", "expert"), scatter_dimension=0, tiled=True),
        lax.psum_scatter(grad_wkey, ("dp", "expert"), scatter_dimension=0, tiled=True),
        lax.psum_scatter(grad_wvalue, ("dp", "expert"), scatter_dimension=0, tiled=True),
        lax.psum_scatter(grad_wout, ("dp", "expert"), scatter_dimension=0, tiled=True),
        lax.psum_scatter(grad_gain_second, ("dp", "expert"), scatter_dimension=0, tiled=True),
        lax.psum_scatter(grad_router, ("dp", "expert"), scatter_dimension=0, tiled=True),
        lax.psum_scatter(grad_sgate, ("dp", "expert"), scatter_dimension=0, tiled=True),
        lax.psum_scatter(grad_sup, ("dp", "expert"), scatter_dimension=0, tiled=True),
        lax.psum_scatter(grad_sdown, ("dp", "expert"), scatter_dimension=0, tiled=True),
    )
    return (
        output,
        grad_inputs,
        summed[0],
        summed[1],
        summed[2],
        summed[3],
        summed[4],
        summed[5],
        summed[6],
        summed[7],
        summed[8],
        summed[9],
        grad_rgate,
        grad_rup,
        grad_rdown,
    )


def solution(mesh):
    placed = (
        P(("dp", "expert"), None),
        P(("dp", "expert"), None),
        P(("dp", "expert"), None),
        P(),
        P(),
        P(),
        P(),
        P(),
        P(),
        P(),
        P(),
        P(),
        P(),
        P(),
        P("expert", None, None),
        P("expert", None, None),
        P("expert", None, None),
    )
    return jax.shard_map(
        shards,
        mesh=mesh,
        in_specs=placed,
        out_specs=(
            P(("dp", "expert"), None),
            P(("dp", "expert"), None),
            P(("dp", "expert")),
            P(("dp", "expert"), None),
            P(("dp", "expert"), None),
            P(("dp", "expert"), None),
            P(("dp", "expert"), None),
            P(("dp", "expert")),
            P(("dp", "expert"), None),
            P(("dp", "expert"), None),
            P(("dp", "expert"), None),
            P(("dp", "expert"), None),
            P("expert", "dp", None),
            P("expert", "dp", None),
            P("expert", "dp", None),
        ),
        check_vma=False,
    )
```

profile of v0, /device:TPU:0, one launch (start us, length us, event | category | flops | bytes accessed | tf_op | source)
XLA Modules:
  0.0 1372.0 jit_solution(2783529125610306192)
XLA Ops:
  17.7 3.5 fusion.89
  26.4 3.5 fusion.87
  44.1 4.1 reshape.266
  48.2 8.7 scatter_custom_fusion
  56.9 6.3 all-to-all-start
  63.2 3.6 mul.576
  66.9 5.1 mul.584
  75.3 12.2 scatter_custom_fusion.1
  87.5 36.1 %all-to-all-done = bf16[8,2,64,1280]{3,2,1,0:T(8,128)(2,1)} async-done(((bf16[8,2,64,1280]{3,2,1,0:T(8,128)(2,1)}), bf16[8,2,64,1280]{3,2,1,0:T(8,128)(2,1)}, u32[]{:S(2)}, u32[]{:S(2)}) %all-to-all-start) | async-done | bytes 2621472 | tf_op jit(solution)/shard_map/all_to_all | solution.py:159
  123.6 4.8 all-to-all-start.2
  128.4 7.8 fusion.3
  136.2 7.8 fusion.7
  144.0 44.7 %all-to-all-done.2 = bf16[8,2,64,1280]{3,2,1,0:T(8,128)(2,1)} async-done(((bf16[8,2,64,1280]{3,2,1,0:T(8,128)(2,1)}), bf16[8,2,64,1280]{3,2,1,0:T(8,128)(2,1)}, u32[]{:S(2)}, u32[]{:S(2)}) %all-to-all-start.2) | async-done | bytes 2621472 | tf_op jit(solution)/shard_map/all_to_all | solution.py:185
  188.7 11.0 fusion.20
  199.8 6.1 fusion.27
  207.6 4.4 all-to-all-start.1
  213.9 58.4 %all-to-all-done.1 = bf16[8,2,64,1280]{3,2,1,0:T(8,128)(2,1)} async-done(((bf16[8,2,64,1280]{3,2,1,0:T(8,128)(2,1)}), bf16[8,2,64,1280]{3,2,1,0:T(8,128)(2,1)}, u32[]{:S(2)}, u32[]{:S(2)}) %all-to-all-start.1) | async-done | bytes 2621472 | tf_op jit(solution)/shard_map/all_to_all | solution.py:169
  272.3 7.3 gather_fusion
  279.6 4.5 reshape.244
  284.1 5.0 multiply_reduce_fusion
  294.1 7.4 bitcast_convert_fusion.2
  301.6 7.3 bitcast_convert_fusion.1
  309.0 7.0 bitcast_convert_fusion
  324.9 4.0 fusion.102
  329.0 5.9 fusion.1
  334.9 5.5 fusion.30
  342.2 4.5 all-to-all-start.3
  351.3 56.5 %all-to-all-done.3 = bf16[8,2,64,1280]{3,2,1,0:T(8,128)(2,1)} async-done(((bf16[8,2,64,1280]{3,2,1,0:T(8,128)(2,1)}), bf16[8,2,64,1280]{3,2,1,0:T(8,128)(2,1)}, u32[]{:S(2)}, u32[]{:S(2)}) %all-to-all-start.3) | async-done | bytes 2621472 | tf_op jit(solution)/shard_map/all_to_all | solution.py:228
  407.8 7.3 gather_fusion.1
  415.1 4.5 reshape.245
  419.6 4.9 reduce_sum.174
  440.8 5.0 fusion.85
  447.8 4.9 fusion.83
  455.1 5.0 fusion.81
  460.4 5.0 fusion.68
  465.4 4.0 fusion.103
  469.4 93.9 %fusion = f32[32,1280]{1,0:T(8,128)S(1)} fusion(f32[896,1280]{1,0:T(8,128)} %fusion.103), kind=kCustom, calls=%all-reduce-scatter | all-reduce-scatter fusion | flops 1310721 | bytes 4751360
  569.9 6.3 collective-permute-start.3
  576.2 4.7 collective-permute-done.3
  580.9 8.1 concatenate.20
  590.8 3.3 fusion.99
  597.5 48.6 %all-reduce.7 = (f32[1280]{0:T(1024)S(1)}, f32[1280]{0:T(1024)S(1)}) all-reduce(f32[1280]{0:T(1024)S(1)} %get-tuple-element.19, f32[1280]{0:T(1024)S(1)} %copy-done.44), channel_id=2, replica_groups=mesh['dp'=4,'expert'=8] {'dp','expert'}, use_global_device_ids=true, to_apply=%region_23.24.clone | all-reduce | flops 2560 | bytes 20480
  647.3 3.3 fusion.35
  661.5 109.6 %reduce-scatter.35.cloned.1.call-done = f32[40,896]{1,0:T(8,128)} async-done(((f32[1280,896]{1,0:T(8,128)}), f32[40,896]{1,0:T(8,128)}) %reduce-scatter.35.cloned.1.call-update) | async-done | bytes 143376
  771.1 148.4 %reduce-scatter.19.cloned.1.call-done = f32[40,1280]{1,0:T(8,128)} async-done(((f32[1280,1280]{1,0:T(8,128)}), f32[40,1280]{1,0:T(8,128)}) %reduce-scatter.19.cloned.1.call-update) | async-done | bytes 204816 | tf_op jit(solution)/shard_map/reduce_scatter | solution.py:307
  919.5 148.4 %reduce-scatter.21.cloned.1.call-done = f32[40,1280]{1,0:T(8,128)} async-done(((f32[1280,1280]{1,0:T(8,128)}), f32[40,1280]{1,0:T(8,128)}) %reduce-scatter.21.cloned.1.call-update) | async-done | bytes 204816 | tf_op jit(solution)/shard_map/reduce_scatter | solution.py:308
  1067.8 147.8 %reduce-scatter.23.cloned.1.call-done = f32[40,1280]{1,0:T(8,128)} async-done(((f32[1280,1280]{1,0:T(8,128)}), f32[40,1280]{1,0:T(8,128)}) %reduce-scatter.23.cloned.1.call-update) | async-done | bytes 204816 | tf_op jit(solution)/shard_map/reduce_scatter | solution.py:309
  1215.7 148.3 %reduce-scatter.25.cloned.1.call-done = f32[40,1280]{1,0:T(8,128)} async-done(((f32[1280,1280]{1,0:T(8,128)}), f32[40,1280]{1,0:T(8,128)}) %reduce-scatter.25.cloned.1.call-update) | async-done | bytes 204816 | tf_op jit(solution)/shard_map/reduce_scatter | solution.py:310
  (221 shorter events, 100.9 us)
Async XLA Ops:
  8.0 5.5 copy-start
  12.2 5.5 copy-start.32
  12.3 35.9 %copy-start.45 = (s32[768]{0:T(1024)}, s32[768]{0:T(1024)S(1)}, u32[]{:S(2)}) copy-start(s32[768]{0:T(1024)S(1)} %fusion.77) | copy-start | bytes 9220
  13.5 12.9 copy-start.37
  37.7 2.9 copy-start.42
  38.4 3.0 copy-start.36
  40.6 7.6 copy-start.49
  56.9 66.7 %all-to-all-start = ((bf16[8,2,64,1280]{3,2,1,0:T(8,128)(2,1)}), bf16[8,2,64,1280]{3,2,1,0:T(8,128)(2,1)}, u32[]{:S(2)}, u32[]{:S(2)}) async-start(bf16[8,2,64,1280]{3,2,1,0:T(8,128)(2,1)} %bitcast.162), calls=%async_computation | async-start | bytes 5242880 | tf_op jit(solution)/shard_map/all_to_all | solution.py:159
  66.9 5.1 copy-start.35
  66.9 6.9 copy-start.41
  66.9 8.4 copy-start.46
  123.6 65.1 %all-to-all-start.2 = ((bf16[8,2,64,1280]{3,2,1,0:T(8,128)(2,1)}), bf16[8,2,64,1280]{3,2,1,0:T(8,128)(2,1)}, u32[]{:S(2)}, u32[]{:S(2)}) async-start(bf16[8,2,64,1280]{3,2,1,0:T(8,128)(2,1)} %bitcast.163), calls=%async_computation.2 | async-start | bytes 5242880 | tf_op jit(solution)/shard_map/all_to_all | solution.py:185
  199.8 6.1 copy-start.52
  207.6 64.7 %all-to-all-start.1 = ((bf16[8,2,64,1280]{3,2,1,0:T(8,128)(2,1)}), bf16[8,2,64,1280]{3,2,1,0:T(8,128)(2,1)}, u32[]{:S(2)}, u32[]{:S(2)}) async-start(bf16[8,2,64,1280]{3,2,1,0:T(8,128)(2,1)} %copy.159), calls=%async_computation.1 | async-start | bytes 5242880 | tf_op jit(solution)/shard_map/all_to_all | solution.py:169
  212.0 439.6 %all-reduce.10.cloned.1.call-start = ((), (), s32[]{:S(2)}) async-start(), calls=%async_computation.20 | async-start | bytes 163840
  213.9 65.6 %copy-start.39 = (s32[1024]{0:T(1024)}, s32[1024]{0:T(1024)S(1)}, u32[]{:S(2)}) copy-start(s32[1024]{0:T(1024)S(1)} %pad_clamp_fusion) | copy-start | bytes 12292
  293.9 359.2 %reduce-scatter.27.cloned.1.call-start = ((), (), s32[]{:S(2)}) async-start(), calls=%async_computation.17 | async-start | bytes 5734400 | tf_op jit(solution)/shard_map/reduce_scatter | solution.py:218
  301.5 354.3 %reduce-scatter.29.cloned.1.call-start = ((), (), s32[]{:S(2)}) async-start(), calls=%async_computation.18 | async-start | bytes 5734400 | tf_op jit(solution)/shard_map/reduce_scatter | solution.py:221
  308.9 349.8 %reduce-scatter.31.cloned.1.call-start = ((), (), s32[]{:S(2)}) async-start(), calls=%async_computation.19 | async-start | bytes 5734400 | tf_op jit(solution)/shard_map/reduce_scatter | solution.py:224
  316.0 345.5 %reduce-scatter.33.cloned.1.call-start = ((), (), s32[]{:S(2)}) async-start(), calls=%async_computation.21 | async-start | bytes 4730880
  316.0 3.4 copy-start.16
  316.0 3.6 copy-start.30
  324.8 446.2 %reduce-scatter.35.cloned.1.call-start = ((), (), s32[]{:S(2)}) async-start(), calls=%async_computation.22 | async-start | bytes 4730880
  329.0 5.9 copy-start.51
  342.2 4.8 copy-start.43
  342.2 65.7 %all-to-all-start.3 = ((bf16[8,2,64,1280]{3,2,1,0:T(8,128)(2,1)}), bf16[8,2,64,1280]{3,2,1,0:T(8,128)(2,1)}, u32[]{:S(2)}, u32[]{:S(2)}) async-start(bf16[8,2,64,1280]{3,2,1,0:T(8,128)(2,1)} %copy.163), calls=%async_computation.3 | async-start | bytes 5242880 | tf_op jit(solution)/shard_map/all_to_all | solution.py:228
  346.7 572.8 %reduce-scatter.19.cloned.1.call-start = ((), (), s32[]{:S(2)}) async-start(), calls=%async_computation.13 | async-start | bytes 6758400 | tf_op jit(solution)/shard_map/reduce_scatter | solution.py:307
  349.7 58.1 %copy-start.40 = (s32[1024]{0:T(1024)S(1)}, s32[1024]{0:T(1024)}, u32[]{:S(2)}) copy-start(s32[1024]{0:T(1024)} %copy-done.39) | copy-start | bytes 12292
  419.6 4.9 copy-start.50
  424.5 3.1 copy-start.7
  424.5 5.2 copy-start.10
  433.5 3.0 copy-start.25
  433.5 3.0 copy-start.27
  433.5 3.3 copy-start.21
  433.5 3.3 copy-start.23
  437.2 3.6 copy-start.38
  445.9 622.0 %reduce-scatter.21.cloned.1.call-start = ((), (), s32[]{:S(2)}) async-start(), calls=%async_computation.14 | async-start | bytes 6758400 | tf_op jit(solution)/shard_map/reduce_scatter | solution.py:308
  452.7 763.0 %reduce-scatter.23.cloned.1.call-start = ((), (), s32[]{:S(2)}) async-start(), calls=%async_computation.15 | async-start | bytes 6758400 | tf_op jit(solution)/shard_map/reduce_scatter | solution.py:309
  460.1 903.8 %reduce-scatter.25.cloned.1.call-start = ((), (), s32[]{:S(2)}) async-start(), calls=%async_computation.16 | async-start | bytes 6758400 | tf_op jit(solution)/shard_map/reduce_scatter | solution.py:310
  563.3 17.6 %collective-permute-start.2 = (f32[32,1280]{1,0:T(8,128)S(1)}, f32[32,1280]{1,0:T(8,128)}, u32[]{:S(2)}, u32[]{:S(2)}) collective-permute-start(f32[32,1280]{1,0:T(8,128)S(1)} %fusion), channel_id=1, source_target_pairs={{0,3},{1,4},{2,5},{3,6},{4,7},{5,8},{6,9},{7,10},{8,11},{9,12},{10... | collective-permute-start | bytes 491528
  565.3 15.6 %collective-permute-start.1 = (f32[32,1280]{1,0:T(8,128)S(1)}, f32[32,1280]{1,0:T(8,128)}, u32[]{:S(2)}, u32[]{:S(2)}) collective-permute-start(f32[32,1280]{1,0:T(8,128)S(1)} %fusion), channel_id=1, source_target_pairs={{0,2},{1,3},{2,4},{3,5},{4,6},{5,7},{6,8},{7,9},{8,10},{9,11},{10,... | collective-permute-start | bytes 491528
  567.2 13.7 collective-permute-start
  569.9 11.0 collective-permute-start.3
  589.0 5.0 copy-start.11
  589.0 5.0 copy-start.19
  646.1 4.5 copy-start.3
  646.1 4.5 copy-start.13
  646.1 4.5 copy-start.28
  (23 other events, 34.7 us)
Sparse Core Ops, SparseCore 0:
  294.0 166.7 all-reduce.9
Sparse Core Ops, SparseCore 1:
  301.6 54.8 reduce-scatter.26
  359.5 55.9 reduce-scatter.28
  418.4 56.0 reduce-scatter.30
  477.3 149.9 reduce-scatter.32
  630.2 140.8 reduce-scatter.34
  774.0 145.4 reduce-scatter.18
  922.2 145.6 reduce-scatter.20
  1070.6 145.0 reduce-scatter.22
  1218.4 145.4 reduce-scatter.24
where the time goes:
time: 1380 us; the launch traced here: 1370 us
  waiting for transfers between devices  903 us (65%)
  blocking collectives  143 us (10%)
  matrix products  138 us (10%)
  local copies, waits for them, and re-layouts  90.9 us (7%)
  other arithmetic  46.8 us (3%)
  starting transfers between devices  33.3 us (2%)
  between operations  17 us (1%)
    reduce_scatter x1, waiting for transfers between devices, shards(): lax.psum_scatter(grad_wkey, ('dp', 'expert'), scatter_dimension=0, tiled=...  148 us
    reduce_scatter x1, waiting for transfers between devices, shards(): lax.psum_scatter(grad_wquery, ('dp', 'expert'), scatter_dimension=0, tile...  148 us
    reduce_scatter x1, waiting for transfers between devices, shards(): lax.psum_scatter(grad_wout, ('dp', 'expert'), scatter_dimension=0, tiled=...  148 us
    reduce_scatter x1, waiting for transfers between devices, shards(): lax.psum_scatter(grad_wvalue, ('dp', 'expert'), scatter_dimension=0, tile...  148 us
    unnamed x2, blocking collectives  143 us
    unnamed x17, waiting for transfers between devices  114 us
    all_to_all x1, waiting for transfers between devices, shards(): lax.all_to_all(expert_result, 'expert', split_axis=0, concat_axis=0, tile...  58.4 us
    all_to_all x1, waiting for transfers between devices, shards(): lax.all_to_all(d_rows, 'expert', split_axis=0, concat_axis=0, tiled=True)  56.5 us
  transfers between devices with their start and end apart: 18, of which 10 were waited for; matrix products, arithmetic and copies ran while one was open for 20% of the time, Pallas kernels for 0%

commit v1 on v0

v1 whole, which is shorter than its diff:
```python
import math

import jax
import jax.numpy as jnp
from jax import lax
from jax.sharding import PartitionSpec as P

HEADS = 10
HEAD_DIM = 128
TOP = 6
LANES = 128
epsilon = 1e-06
BF = jnp.bfloat16
F32 = jnp.float32


def rotary_tables(length, half_width):
    position = jnp.arange(length, dtype=jnp.float32)[:, None]
    frequencies = jnp.exp(
        jnp.arange(half_width, dtype=jnp.float32) * (-math.log(10000.0) / half_width)
    )
    angles = position * frequencies[None, :]
    return (jnp.cos(angles)[:, None, :], jnp.sin(angles)[:, None, :])


def rotate(operand, cosine, sine_table, direction):
    half_width = operand.shape[-1] // 2
    first_half = operand[..., :half_width]
    second = operand[..., half_width:]
    return jnp.concatenate(
        [
            first_half * cosine - direction * second * sine_table,
            second * cosine + direction * first_half * sine_table,
        ],
        -1,
    )


def product(left, right):
    return jnp.dot(left, right, preferred_element_type=jnp.float32)


def product_right(left, right):
    return lax.dot_general(
        left, right, (((1,), (1,)), ((), ())), preferred_element_type=jnp.float32
    )


def norm_backward(grad_normed, unit_rows, row_scale, gain):
    scaled_grad = grad_normed * gain
    grad_gain = jnp.sum(grad_normed * unit_rows, 0)
    grad_rows = row_scale * (
        scaled_grad - unit_rows * jnp.mean(scaled_grad * unit_rows, -1, keepdims=True)
    )
    return (grad_rows, grad_gain)


def partner(v, axis, mask):
    n = lax.axis_size(axis)
    return lax.ppermute(v, axis, [(i, i ^ mask) for i in range(n)])


def plus(a, b):
    return (a.astype(F32) + b.astype(F32)).astype(BF)


def gather_expert(v):
    pairs = lax.axis_size("expert") // 2
    mine = jnp.stack([v] + [partner(v, "expert", 2 * k) for k in range(1, pairs)])
    return jnp.stack([mine, partner(mine, "expert", 1)])


def reduce_z(s):
    total = s[0].astype(F32)
    for k in range(1, s.shape[0]):
        total = total + partner(s[k], "expert", 2 * k).astype(F32)
    return total


def reduce_expert(y):
    return reduce_z(plus(y[0], partner(y[1], "expert", 1)))


def reduce_dp(g, masks):
    n = g.shape[0]
    left = list(range(n))
    parts = {r: g[r] for r in left}
    for mask in masks:
        keep = [r for r in left if not r & mask]
        sent = jnp.stack([parts[r ^ mask] for r in keep])
        got = partner(sent, "dp", mask)
        parts = {r: plus(parts[r], got[i]) for i, r in enumerate(keep)}
        left = keep
    return parts[0]


def dp_masks():
    n = lax.axis_size("dp")
    return [1 << b for b in range(n.bit_length() - 1)]


def reduce_rest(g):
    cols = g.shape[-1]
    half = cols // 2 // LANES * LANES
    up = dp_masks()
    a = reduce_dp(g[..., :half], up)
    b = reduce_dp(g[..., half:], up[::-1])
    return jnp.concatenate([reduce_z(a), reduce_z(b)], -1)


def relative_rows(d):
    n_dp, n_ex = lax.axis_size("dp"), lax.axis_size("expert")
    n = n_dp * n_ex
    rows = d // n
    me = lax.axis_index("dp") * n_ex + lax.axis_index("expert")
    i = jnp.arange(d, dtype=jnp.int32)
    half = i // (d // 2)
    block = (i % (d // 2)) // rows * 2 + half
    source = (me ^ block) * rows + i % rows
    return (source[:, None] == jnp.arange(d, dtype=jnp.int32)[None, :]).astype(BF)


def split_rows(x, order):
    return product_right(order, x).astype(BF).reshape(2, x.shape[1] // 2, x.shape[0])


def pair_rows(x, order):
    xt = split_rows(x, order)
    return jnp.concatenate([xt[0], partner(xt[1], "expert", 1)], -1)


def pair_tokens(v):
    return jnp.concatenate([v, partner(v, "expert", 1)], 0)


def weight_grad(xt, dy):
    n_dp, n_z = lax.axis_size("dp"), lax.axis_size("expert") // 2
    g = product(xt, dy).astype(BF)
    return g.reshape(n_dp, n_z, -1, dy.shape[1])


def shards(
    tokens,
    cotangent,
    routes,
    expert_at,
    norm1_gain,
    w_query,
    w_key,
    w_value,
    w_out,
    norm2_gain,
    w_router,
    shared_gate,
    shared_up,
    shared_down,
    routed_gate,
    routed_up,
    routed_down,
):
    length, model_width = tokens.shape
    expert_count = w_router.shape[1]
    slot_count = expert_at.shape[0]
    slot_dev = routed_gate.shape[0]
    n_ex = lax.axis_size("expert")
    n_dp = lax.axis_size("dp")
    capacity = (length * TOP * 5 // (4 * expert_count) + 7) // 8 * 8
    score_scale = 1.0 / math.sqrt(HEAD_DIM)
    expert_ids = jnp.arange(expert_count, dtype=jnp.int32)
    order_d = relative_rows(model_width)

    routes_low = jnp.pad(routes.astype(BF), ((0, 0), (0, LANES - TOP)))
    early = gather_expert(jnp.concatenate([cotangent, routes_low], 1))
    early = early.reshape(n_ex, length, model_width + LANES)
    all_dy = early[:, :, :model_width]
    all_routes = early[:, :, model_width : model_width + TOP].astype(jnp.int32)

    inputs_f = tokens.astype(jnp.float32)
    scale_first = lax.rsqrt(jnp.mean(inputs_f * inputs_f, -1, keepdims=True) + epsilon)
    unit_first = inputs_f * scale_first
    normed_first = (unit_first * norm1_gain).astype(jnp.bfloat16)
    cosine, sine_table = rotary_tables(length, HEAD_DIM // 2)

    def heads_of(weight):
        return product(normed_first, weight).reshape(length, HEADS, HEAD_DIM)

    queries = rotate(heads_of(w_query), cosine, sine_table, 1.0).astype(jnp.bfloat16)
    key_heads = rotate(heads_of(w_key), cosine, sine_table, 1.0).astype(jnp.bfloat16)
    value_heads = heads_of(w_value).astype(jnp.bfloat16)
    causal = jnp.arange(length)[:, None] >= jnp.arange(length)[None, :]

    def masked_scores():
        raw_scores = (
            jnp.einsum("qhd,khd->hqk", queries, key_heads, preferred_element_type=jnp.float32)
            * score_scale
        )
        return jnp.where(causal[None], raw_scores, -1e30)

    scores_fwd = masked_scores()
    row_max = jnp.max(scores_fwd, -1, keepdims=True)
    expo_terms = jnp.exp(scores_fwd - row_max)
    row_total = jnp.sum(expo_terms, -1, keepdims=True)
    log_total = row_max + jnp.log(row_total)
    probs_low = (expo_terms / row_total).astype(jnp.bfloat16)
    attended = (
        jnp.einsum("hqk,khd->qhd", probs_low, value_heads, preferred_element_type=jnp.float32)
        .reshape(length, model_width)
        .astype(jnp.bfloat16)
    )
    residual = inputs_f + product(attended, w_out)
    scale_second = lax.rsqrt(jnp.mean(residual * residual, -1, keepdims=True) + epsilon)
    unit_second = residual * scale_second
    normed_second = (unit_second * norm2_gain).astype(jnp.bfloat16)

    all_normed = gather_expert(normed_second).reshape(n_ex, length, model_width)

    shared_g = product(normed_second, shared_gate)
    shared_u = product(normed_second, shared_up)
    shared_sigmoid = jax.nn.sigmoid(shared_g)
    shared_act = shared_g * shared_sigmoid
    shared_hidden = (shared_act * shared_u).astype(jnp.bfloat16)
    shared_result = product(shared_hidden, shared_down)
    grad_output = cotangent.astype(jnp.float32)
    d_shared = cotangent
    d_shared_hidden = product_right(d_shared, shared_down)
    d_shared_g = (
        d_shared_hidden * shared_u * shared_sigmoid * (1.0 + shared_g * (1.0 - shared_sigmoid))
    ).astype(jnp.bfloat16)
    d_shared_u = (d_shared_hidden * shared_act).astype(jnp.bfloat16)
    normed_second_t = pair_rows(normed_second, order_d)
    shared_part = weight_grad(
        normed_second_t, pair_tokens(jnp.concatenate([d_shared_g, d_shared_u], 1))
    )
    down_part = weight_grad(pair_rows(shared_hidden, relative_rows(shared_hidden.shape[1])), pair_tokens(d_shared))
    grad_sgu = reduce_rest(shared_part)
    grad_sdown = reduce_rest(down_part)
    ff = shared_gate.shape[1]
    grad_sgate, grad_sup = grad_sgu[:, :ff], grad_sgu[:, ff:]

    def router_of(rows):
        logits = product(rows, w_router)
        logit_terms = jnp.exp(logits - jnp.max(logits, -1, keepdims=True))
        return logit_terms / jnp.sum(logit_terms, -1, keepdims=True)

    router_probs = router_of(normed_second)

    my_expert = lax.dynamic_slice_in_dim(
        expert_at, lax.axis_index("expert") * slot_dev, slot_dev
    )
    member = jnp.sum(
        (all_routes[None] == my_expert[:, None, None, None]).astype(F32), -1
    )
    place = jnp.arange(length)
    earlier = (place[:, None] < place[None, :]).astype(BF)
    position = jnp.einsum("snt,tv->snv", member.astype(BF), earlier, preferred_element_type=F32)
    row_ids = jnp.arange(capacity, dtype=jnp.int32)
    pick = (
        (position.astype(jnp.int32)[:, :, None, :] == row_ids[None, None, :, None])
        & (member[:, :, None, :] > 0.5)
    )
    pick_low = pick.astype(BF)
    all_probs = router_of(all_normed)
    slot_probs = jnp.einsum(
        "nte,se->snt", all_probs, (my_expert[:, None] == expert_ids[None, :]).astype(F32),
        precision=lax.Precision.HIGHEST,
    )
    row_gate = jnp.sum(jnp.where(pick, slot_probs[:, :, None, :], 0.0), -1)
    row_gate = row_gate.reshape(slot_dev, n_ex * capacity)

    def rows_of(table):
        return (
            jnp.einsum("snrt,ntd->snrd", pick_low, table, preferred_element_type=F32)
            .astype(BF)
            .reshape(slot_dev, n_ex * capacity, model_width)
        )

    x_rows = rows_of(all_normed)
    dy_rows = rows_of(all_dy)
    d_result = (row_gate[:, :, None] * dy_rows.astype(F32)).astype(BF)
    expert_g = jnp.einsum("srd,sdf->srf", x_rows, routed_gate, preferred_element_type=F32)
    expert_u = jnp.einsum("srd,sdf->srf", x_rows, routed_up, preferred_element_type=F32)
    sigmoid_gate = jax.nn.sigmoid(expert_g)
    activated = expert_g * sigmoid_gate
    expert_hidden = (activated * expert_u).astype(BF)
    expert_result = jnp.einsum(
        "srf,sfd->srd", expert_hidden, routed_down, preferred_element_type=F32
    ).astype(BF)
    d_hidden = jnp.einsum("srd,sfd->srf", d_result, routed_down, preferred_element_type=F32)
    d_expert_g = (
        d_hidden * expert_u * sigmoid_gate * (1.0 + expert_g * (1.0 - sigmoid_gate))
    ).astype(BF)
    d_expert_u = (d_hidden * activated).astype(BF)
    d_rows = (
        jnp.einsum("srf,sdf->srd", d_expert_g, routed_gate, preferred_element_type=F32)
        + jnp.einsum("srf,sdf->srd", d_expert_u, routed_up, preferred_element_type=F32)
    ).astype(BF)
    row_d_gate = jnp.sum(dy_rows.astype(F32) * expert_result.astype(F32), -1)
    scaled = (row_gate[:, :, None] * expert_result.astype(F32)).astype(BF)

    def tokens_of(rows):
        return jnp.einsum(
            "snrt,snrd->ntd",
            pick_low,
            rows.reshape(slot_dev, n_ex, capacity, model_width),
            preferred_element_type=F32,
        ).astype(BF)

    d_gate_tokens = jnp.sum(
        jnp.where(pick, row_d_gate.reshape(slot_dev, n_ex, capacity)[..., None], 0.0), 2
    )
    wide_ids = jnp.arange(LANES, dtype=jnp.int32)
    d_gate_cols = jnp.sum(
        jnp.where(
            my_expert[:, None, None, None] == wide_ids[None, None, None, :],
            d_gate_tokens[..., None],
            0.0,
        ),
        0,
    ).astype(BF)
    back = jnp.concatenate([tokens_of(d_rows), d_gate_cols], -1)
    back = reduce_expert(back.reshape(2, n_ex // 2, length, -1))
    routed_grad, d_probs = back[:, :model_width], back[:, model_width : model_width + expert_count]
    combined = reduce_expert(tokens_of(scaled).reshape(2, n_ex // 2, length, -1))
    output = (residual + shared_result + combined).astype(BF)

    my_dp = lax.axis_index("dp")

    def routed_grad_of(left, right):
        width = left.shape[-1]
        left_t = jnp.swapaxes(left, 1, 2).reshape(slot_dev, n_dp, width // n_dp, -1)
        left_t = jnp.concatenate(
            [lax.dynamic_slice_in_dim(left_t, my_dp ^ q, 1, 1) for q in range(n_dp)], 1
        )
        return jnp.einsum("sqdr,srf->sqdf", left_t, right, preferred_element_type=F32).astype(BF)

    rg_part = routed_grad_of(x_rows, d_expert_g)
    ru_part = routed_grad_of(x_rows, d_expert_u)
    rd_part = routed_grad_of(expert_hidden, d_result)
    up_masks = dp_masks()

    def reduce_slots(part):
        return jnp.stack(
            [
                reduce_dp(part[s], up_masks if s % 2 == 0 else up_masks[::-1]).astype(F32)
                for s in range(slot_dev)
            ]
        )

    grad_rgate, grad_rup, grad_rdown = reduce_slots(rg_part), reduce_slots(ru_part), reduce_slots(rd_part)

    d_logits = (
        router_probs * (d_probs - jnp.sum(router_probs * d_probs, -1, keepdims=True))
    ).astype(jnp.bfloat16)
    d_normed_second = (
        product_right(d_shared_g, shared_gate)
        + product_right(d_shared_u, shared_up)
        + product_right(d_logits, w_router)
        + routed_grad
    )
    d_second, grad_gain_second = norm_backward(
        d_normed_second, unit_second, scale_second, norm2_gain
    )
    d_residual = grad_output + d_second
    d_branch = d_residual.astype(jnp.bfloat16)
    out_part = weight_grad(pair_rows(attended, order_d), pair_tokens(d_branch))
    grad_wout = reduce_rest(out_part)
    d_attended = (
        product_right(d_branch, w_out).astype(jnp.bfloat16).reshape(length, HEADS, HEAD_DIM)
    )
    att_probs = jnp.exp(masked_scores() - log_total)
    d_att = jnp.einsum("qhd,khd->hqk", d_attended, value_heads, preferred_element_type=jnp.float32)
    d_scores = (att_probs * (d_att - jnp.sum(att_probs * d_att, -1, keepdims=True))).astype(
        jnp.bfloat16
    )
    d_values = (
        jnp.einsum(
            "hqk,qhd->khd",
            att_probs.astype(jnp.bfloat16),
            d_attended,
            preferred_element_type=jnp.float32,
        )
        .astype(jnp.bfloat16)
        .reshape(length, model_width)
    )
    d_query_rot = (
        jnp.einsum("hqk,khd->qhd", d_scores, key_heads, preferred_element_type=jnp.float32)
        * score_scale
    )
    d_key_rot = (
        jnp.einsum("hqk,qhd->khd", d_scores, queries, preferred_element_type=jnp.float32)
        * score_scale
    )
    d_queries = (
        rotate(d_query_rot, cosine, sine_table, -1.0)
        .astype(jnp.bfloat16)
        .reshape(length, model_width)
    )
    d_keys = (
        rotate(d_key_rot, cosine, sine_table, -1.0)
        .astype(jnp.bfloat16)
        .reshape(length, model_width)
    )
    normed_first_t = pair_rows(normed_first, order_d)
    qkv_part = weight_grad(
        normed_first_t, pair_tokens(jnp.concatenate([d_queries, d_keys, d_values], 1))
    )
    d_normed_first = (
        product_right(d_queries, w_query)
        + product_right(d_keys, w_key)
        + product_right(d_values, w_value)
    )
    d_first, grad_gain_first = norm_backward(d_normed_first, unit_first, scale_first, norm1_gain)
    grad_inputs = d_residual + d_first
    small_rows = weight_grad(
        normed_second_t,
        pair_tokens(jnp.pad(d_logits, ((0, 0), (0, LANES - expert_count)))),
    )
    gains = jnp.stack([grad_gain_first, grad_gain_second], 0).astype(BF)
    gains = split_rows(gains, order_d).reshape(2, n_dp, n_ex // 2, -1, 2)
    gains = plus(gains[0], partner(gains[1], "expert", 1))
    gains = jnp.pad(gains, ((0, 0),) * 3 + ((0, LANES - 2),))
    last = reduce_rest(jnp.concatenate([qkv_part, small_rows, gains], -1))
    w = model_width
    return (
        output,
        grad_inputs,
        last[:, 3 * w + LANES],
        last[:, :w],
        last[:, w : 2 * w],
        last[:, 2 * w : 3 * w],
        grad_wout,
        last[:, 3 * w + LANES + 1],
        last[:, 3 * w : 3 * w + expert_count],
        grad_sgate,
        grad_sup,
        grad_sdown,
        grad_rgate,
        grad_rup,
        grad_rdown,
    )


def solution(mesh):
    placed = (
        P(("dp", "expert"), None),
        P(("dp", "expert"), None),
        P(("dp", "expert"), None),
        P(),
        P(),
        P(),
        P(),
        P(),
        P(),
        P(),
        P(),
        P(),
        P(),
        P(),
        P("expert", None, None),
        P("expert", None, None),
        P("expert", None, None),
    )
    return jax.shard_map(
        shards,
        mesh=mesh,
        in_specs=placed,
        out_specs=(
            P(("dp", "expert"), None),
            P(("dp", "expert"), None),
            P(("dp", "expert")),
            P(("dp", "expert"), None),
            P(("dp", "expert"), None),
            P(("dp", "expert"), None),
            P(("dp", "expert"), None),
            P(("dp", "expert")),
            P(("dp", "expert"), None),
            P(("dp", "expert"), None),
            P(("dp", "expert"), None),
            P(("dp", "expert"), None),
            P("expert", "dp", None),
            P("expert", "dp", None),
            P("expert", "dp", None),
        ),
        check_vma=False,
    )
```

time: 1380 us -> 566 us (0.41)
  waiting for transfers between devices: 903 us -> 179 us
  blocking collectives: 143 us -> 0 us
  starting transfers between devices: 33.3 us -> 104 us
  other arithmetic: 46.8 us -> 84.4 us
  matrix products: 138 us -> 111 us
  local copies, waits for them, and re-layouts: 90.9 us -> 74.2 us
  between operations: 17 us -> 2.73 us
    reduce_scatter x7 -> x0, waiting for transfers between devices: 593 us -> none  [the longest x1 148 us: shards(): lax.psum_scatter(grad_wkey, ('dp', 'expert'), scatter_dimension=0, tiled=...]
    all_to_all x4 -> x0, waiting for transfers between devices: 196 us -> none  [the longest x1 58.4 us: shards(): lax.all_to_all(expert_result, 'expert', split_axis=0, concat_axis=0, tile...]
    ppermute x0 -> x78, waiting for transfers between devices: none -> 179 us  [partner(): return lax.ppermute(v, axis, [(i, i ^ mask) for i in range(n)])]
    unnamed x2 -> x0, blocking collectives: 143 us -> none
    unnamed x17 -> x0, waiting for transfers between devices: 114 us -> none
    ppermute x0 -> x78, starting transfers between devices: none -> 104 us  [partner(): return lax.ppermute(v, axis, [(i, i ^ mask) for i in range(n)])]
    dot_general x17 -> x15, matrix products: 98.4 us -> 47.8 us  [the longest x3 8.74 us: routed_grad_of(): jnp.einsum('sqdr,srf->sqdf', left_t, right, preferred_element_type=F32)]
    another operation x5 -> x21, other arithmetic: 4.45 us -> 29.8 us  [the longest x4 11.6 us: gather_expert(): return jnp.stack([mine, partner(mine, 'expert', 1)])]
  transfers between devices with their start and end apart: 18 -> 78, of which waited for: 10 -> 29; matrix products, arithmetic and copies ran while one was open for 20% -> 31% of each run, Pallas kernels for 0% -> 0%
where the time goes in v1:
time: 566 us; the launch traced here: 555 us
  waiting for transfers between devices  179 us (32%)
  matrix products  111 us (20%)
  starting transfers between devices  104 us (18%)
  other arithmetic  84.4 us (15%)
  local copies, waits for them, and re-layouts  74.2 us (13%)
    ppermute x78, waiting for transfers between devices, partner(): return lax.ppermute(v, axis, [(i, i ^ mask) for i in range(n)])  179 us
    ppermute x78, starting transfers between devices, partner(): return lax.ppermute(v, axis, [(i, i ^ mask) for i in range(n)])  104 us
    dot_general x13, matrix products, product(): return jnp.dot(left, right, preferred_element_type=jnp.float32)  29.4 us
    unnamed x221, local copies, waits for them, and re-layouts  29.4 us
    dot_general x13, matrix products, product_right(): lax.dot_general(left, right, (((1,), (1,)), ((), ())), preferred_element_...  24.5 us
    convert_element_type x25, other arithmetic, plus(): return (a.astype(F32) + b.astype(F32)).astype(BF)  23 us
    another operation x4, other arithmetic, gather_expert(): return jnp.stack([mine, partner(mine, 'expert', 1)])  11.6 us
  transfers between devices with their start and end apart: 78, of which 29 were waited for; matrix products, arithmetic and copies ran while one was open for 31% of the time, Pallas kernels for 0%

profile of v1, /device:TPU:0, one launch (start us, length us, event | category | flops | bytes accessed | tf_op | source)
XLA Modules:
  0.0 555.2 jit_solution(4408671407475721386)
XLA Ops:
  3.9 3.6 fusion.223
  12.5 3.6 fusion.221
  34.5 3.0 collective-permute-start.4
  45.2 3.3 fusion.26
  51.5 2.7 fusion.25
  76.5 3.5 collective-permute-start.1
  80.0 3.0 fusion.226
  92.2 12.1 %collective-permute-done.1 = bf16[128,1408]{1,0:T(8,128)(2,1)} collective-permute-done((bf16[128,1408]{1,0:T(8,128)(2,1)}, bf16[128,1408]{1,0:T(8,128)(2,1)}, u32[]{:S(2)}, u32[]{:S(2)}) %collective-permute-start.1) | collective-permute-done | bytes 360480 | tf_op jit(solution)/shard_map/ppermute | solution.py:60
  106.0 3.1 fusion.227
  115.1 3.3 collective-permute-done.57
  120.2 6.7 %collective-permute-start.58 = (bf16[28,640]{1,0:T(8,128)(2,1)S(1)}, bf16[28,640]{1,0:T(8,128)(2,1)S(1)}, u32[]{:S(2)}, u32[]{:S(2)}) collective-permute-start(bf16[28,640]{1,0:T(8,128)(2,1)S(1)} %get-tuple-element.228), channel_id=1, source_target_pairs={{0,2},{1,3},{2,0},{3,1},{4,6},{5,7},{6,4},{7,5},{8,10},{9,11},{10,... | collective-permute-start | bytes 107528 | tf_op jit(solution)/shard_map/ppermute | solution.py:60
  132.2 7.2 %collective-permute-start.63 = (bf16[28,640]{1,0:T(8,128)(2,1)S(1)}, bf16[28,640]{1,0:T(8,128)(2,1)S(1)}, u32[]{:S(2)}, u32[]{:S(2)}) collective-permute-start(bf16[28,640]{1,0:T(8,128)(2,1)S(1)} %get-tuple-element.231), channel_id=1, source_target_pairs={{0,2},{1,3},{2,0},{3,1},{4,6},{5,7},{6,4},{7,5},{8,10},{9,11},{10,... | collective-permute-start | bytes 107528 | tf_op jit(solution)/shard_map/ppermute | solution.py:60
  145.8 2.8 collective-permute-done.50
  167.0 3.4 fusion.242
  173.1 3.7 pad_maximum_fusion
  176.8 5.8 %copy.286 = bf16[2,4,128,1408]{2,1,0,3:T(4,128)(2,1)} copy(bf16[2,4,128,1408]{3,2,1,0:T(8,128)(2,1)} %pad_maximum_fusion) | data formatting | bytes 5767168 | tf_op jit(solution)/shard_map/stack | solution.py:70
  188.4 3.7 slice-done.2
  192.2 2.9 fusion.248
  195.1 4.3 fusion.10
  199.4 8.0 %fusion.7 = (f32[2,512]{1,0:T(2,128)S(1)}, bf16[2,512,1280]{2,1,0:T(8,128)(2,1)}) fusion(f32[2,8,64,1280]{3,2,1,0:T(8,128)S(1)} %copy.299, bf16[2,896,1280]{2,1,0:T(8,128)(2,1)S(1)} %bitcast.401, f32[2,512,896]{2,1,0:T(8,128)S(1)} %get-tuple-element.260, f32[2,512,896]{2,1,0:T(8,128)} %copy-done.93), kind=kOutput, calls=%fused_computation.12 | convolution fusion | flops 2359557120 | bytes 19795968 | tf_op jit(solution)/shard_map/srf,sfd->srd/dot_general | solution.py:285
  208.1 3.6 copy.325
  211.6 5.7 %fusion.9 = (bf16[2,512,1280]{2,1,0:T(8,128)(2,1)S(1)}, bf16[2,512,1280]{2,1,0:T(8,128)(2,1)}) fusion(f32[2,8,64,1280]{3,2,1,0:T(8,128)} %copy-done.9, f32[2,512]{1,0:T(2,128)S(1)} %mul.549, bf16[2,512,1280]{2,1,0:T(8,128)(2,1)} %get-tuple-element.250), kind=kLoop, calls=%fused_computation.16 | loop fusion | flops 6553600 | bytes 13111296 | tf_op jit(solution)/shard_map/convert_element_type | solution.py:279
  217.7 7.7 %multiply_convert_fusion = (bf16[2,512,896]{2,1,0:T(8,128)(2,1)}, bf16[2,512,896]{2,1,0:T(8,128)(2,1)}) fusion(f32[2,512,896]{2,1,0:T(8,128)S(1)} %copy-done.94, f32[2,512,896]{2,1,0:T(8,128)S(1)} %copy-done.96, bf16[2,512,1280]{2,1,0:T(8,128)(2,1)S(1)} %get-tuple-element.240, bf16[2,896,1280]{2,1,0:T(8,128)(2,1)} %param.33), kind=kOutput, calls=%fused_computation.31 | convolution fusion | flops 2360737792 | bytes 18219008 | tf_op jit(solution)/shard_map/srd,sfd->srf/dot_general | solution.py:288
  234.5 4.4 copy.324
  241.2 4.8 fusion.250
  246.0 3.1 convolution_convert_fusion.9
  249.1 3.1 convolution_convert_fusion.8
  260.1 3.5 add_convert_fusion
  278.7 5.6 %collective-permute-done.70 = bf16[2,320,896]{2,1,0:T(8,128)(2,1)} collective-permute-done((bf16[2,320,896]{2,1,0:T(8,128)(2,1)}, bf16[2,320,896]{2,1,0:T(8,128)(2,1)}, u32[]{:S(2)}, u32[]{:S(2)}) %collective-permute-start.70) | collective-permute-done | bytes 1146912 | tf_op jit(solution)/shard_map/ppermute | solution.py:60
  286.5 18.8 %collective-permute-done.66 = bf16[2,320,896]{2,1,0:T(8,128)(2,1)} collective-permute-done((bf16[2,320,896]{2,1,0:T(8,128)(2,1)}, bf16[2,320,896]{2,1,0:T(8,128)(2,1)}, u32[]{:S(2)}, u32[]{:S(2)}) %collective-permute-start.66) | collective-permute-done | bytes 1146912 | tf_op jit(solution)/shard_map/ppermute | solution.py:60
  310.7 17.8 %collective-permute-done.10 = bf16[128,1280]{0,1:T(8,128)(2,1)S(1)} collective-permute-done((bf16[128,1280]{0,1:T(8,128)(2,1)S(1)}, bf16[128,1280]{0,1:T(8,128)(2,1)S(1)}, u32[]{:S(2)}, u32[]{:S(2)}) %collective-permute-start.10) | collective-permute-done | bytes 327712 | tf_op jit(solution)/shard_map/ppermute | solution.py:60
  331.2 6.8 %collective-permute-done.9 = bf16[128,1280]{0,1:T(8,128)(2,1)S(1)} collective-permute-done((bf16[128,1280]{0,1:T(8,128)(2,1)S(1)}, bf16[128,1280]{0,1:T(8,128)(2,1)S(1)}, u32[]{:S(2)}, u32[]{:S(2)}) %collective-permute-start.9) | collective-permute-done | bytes 327712 | tf_op jit(solution)/shard_map/ppermute | solution.py:60
  343.2 3.2 add_convert_fusion.10
  348.6 21.6 %collective-permute-done.71 = bf16[1,320,896]{2,1,0:T(8,128)(2,1)} collective-permute-done((bf16[1,320,896]{2,1,0:T(8,128)(2,1)}, bf16[1,320,896]{2,1,0:T(8,128)(2,1)}, u32[]{:S(2)}, u32[]{:S(2)}) %collective-permute-start.71) | collective-permute-done | bytes 573472 | tf_op jit(solution)/shard_map/ppermute | solution.py:60
  372.2 3.2 add_convert_fusion.12
  375.4 6.0 %collective-permute-done.67 = bf16[1,320,896]{2,1,0:T(8,128)(2,1)S(1)} collective-permute-done((bf16[1,320,896]{2,1,0:T(8,128)(2,1)}, bf16[1,320,896]{2,1,0:T(8,128)(2,1)S(1)}, u32[]{:S(2)}, u32[]{:S(2)}) %collective-permute-start.67) | collective-permute-done | bytes 573472 | tf_op jit(solution)/shard_map/ppermute | solution.py:60
  381.5 3.0 add_convert_fusion.14
  390.9 2.9 convolution_convert_fusion.10
  406.2 3.3 fusion.251
  426.7 10.6 %collective-permute-done.73 = bf16[1,320,896]{2,1,0:T(8,128)(2,1)S(1)} collective-permute-done((bf16[1,320,896]{2,1,0:T(8,128)(2,1)}, bf16[1,320,896]{2,1,0:T(8,128)(2,1)S(1)}, u32[]{:S(2)}, u32[]{:S(2)}) %collective-permute-start.73) | collective-permute-done | bytes 573472 | tf_op jit(solution)/shard_map/ppermute | solution.py:60
  442.5 7.1 %collective-permute-done.69 = bf16[1,320,896]{2,1,0:T(8,128)(2,1)S(1)} collective-permute-done((bf16[1,320,896]{2,1,0:T(8,128)(2,1)}, bf16[1,320,896]{2,1,0:T(8,128)(2,1)S(1)}, u32[]{:S(2)}, u32[]{:S(2)}) %collective-permute-start.69) | collective-permute-done | bytes 573472 | tf_op jit(solution)/shard_map/ppermute | solution.py:60
  452.6 5.2 collective-permute-done.33
  464.6 6.6 %collective-permute-start.35 = (bf16[40,640]{1,0:T(8,128)(2,1)S(1)}, bf16[40,640]{1,0:T(8,128)(2,1)S(1)}, u32[]{:S(2)}, u32[]{:S(2)}) collective-permute-start(bf16[40,640]{1,0:T(8,128)(2,1)S(1)} %get-tuple-element.222), channel_id=1, source_target_pairs={{0,2},{1,3},{2,0},{3,1},{4,6},{5,7},{6,4},{7,5},{8,10},{9,11},{10,... | collective-permute-start | bytes 153608 | tf_op jit(solution)/shard_map/ppermute | solution.py:60
  476.3 4.1 fusion.8
  493.0 16.0 %collective-permute-done.21 = bf16[2,4,40,2048]{3,2,1,0:T(8,128)(2,1)S(1)} collective-permute-done((bf16[2,4,40,2048]{3,2,1,0:T(8,128)(2,1)S(1)}, bf16[2,4,40,2048]{3,2,1,0:T(8,128)(2,1)S(1)}, u32[]{:S(2)}, u32[]{:S(2)}) %collective-permute-start.21) | collective-permute-done | bytes 1310752 | tf_op jit(solution)/shard_map/ppermute | solution.py:60
  513.7 11.2 %collective-permute-done.22 = bf16[1,4,40,2048]{3,2,1,0:T(8,128)(2,1)S(1)} collective-permute-done((bf16[1,4,40,2048]{3,2,1,0:T(8,128)(2,1)S(1)}, bf16[1,4,40,2048]{3,2,1,0:T(8,128)(2,1)S(1)}, u32[]{:S(2)}, u32[]{:S(2)}) %collective-permute-start.22) | collective-permute-done | bytes 655392 | tf_op jit(solution)/shard_map/ppermute | solution.py:60
  536.7 4.7 collective-permute-done.24
  542.1 11.2 %collective-permute-done.29 = bf16[40,2048]{1,0:T(8,128)(2,1)S(1)} collective-permute-done((bf16[40,2048]{1,0:T(8,128)(2,1)S(1)}, bf16[40,2048]{1,0:T(8,128)(2,1)S(1)}, u32[]{:S(2)}, u32[]{:S(2)}) %collective-permute-start.29) | collective-permute-done | bytes 163872 | tf_op jit(solution)/shard_map/ppermute | solution.py:60
  (531 shorter events, 258.0 us)
Async XLA Ops:
  34.5 42.0 %collective-permute-start.4 = (bf16[128,1280]{0,1:T(8,128)(2,1)}, bf16[128,1280]{0,1:T(8,128)(2,1)}, u32[]{:S(2)}, u32[]{:S(2)}) collective-permute-start(bf16[128,1280]{0,1:T(8,128)(2,1)} %multiply_convert_fusion.5), channel_id=1, source_target_pairs={{0,2},{1,3},{2,0},{3,1},{4,6},{5,7},{6,4},{7,5},{8,10},{9,11},{10,... | collective-permute-start | bytes 983048 | tf_op jit(solution)/shard_map/ppermute | solution.py:60
  37.5 42.4 %collective-permute-start.5 = (bf16[128,1280]{0,1:T(8,128)(2,1)}, bf16[128,1280]{0,1:T(8,128)(2,1)}, u32[]{:S(2)}, u32[]{:S(2)}) collective-permute-start(bf16[128,1280]{0,1:T(8,128)(2,1)} %multiply_convert_fusion.5), channel_id=1, source_target_pairs={{0,4},{1,5},{2,6},{3,7},{4,0},{5,1},{6,2},{7,3},{8,12},{9,13},{10,... | collective-permute-start | bytes 983048 | tf_op jit(solution)/shard_map/ppermute | solution.py:60
  40.1 39.8 %collective-permute-start.6 = (bf16[128,1280]{0,1:T(8,128)(2,1)}, bf16[128,1280]{0,1:T(8,128)(2,1)}, u32[]{:S(2)}, u32[]{:S(2)}) collective-permute-start(bf16[128,1280]{0,1:T(8,128)(2,1)} %multiply_convert_fusion.5), channel_id=1, source_target_pairs={{0,6},{1,7},{2,4},{3,5},{4,2},{5,3},{6,0},{7,1},{8,14},{9,15},{10,... | collective-permute-start | bytes 983048 | tf_op jit(solution)/shard_map/ppermute | solution.py:60
  40.1 43.4 %collective-permute-start.55 = (bf16[128,1280]{1,0:T(8,128)(2,1)}, bf16[128,1280]{1,0:T(8,128)(2,1)}, u32[]{:S(2)}, u32[]{:S(2)}) collective-permute-start(bf16[128,1280]{1,0:T(8,128)(2,1)} %param.18), channel_id=1, source_target_pairs={{0,1},{1,0},{2,3},{3,2},{4,5},{5,4},{6,7},{7,6},{8,9},{9,8},{10,11... | collective-permute-start | bytes 983048 | tf_op jit(solution)/shard_map/ppermute | solution.py:60
  42.2 48.3 %collective-permute-start = (bf16[128,1408]{1,0:T(8,128)(2,1)}, bf16[128,1408]{1,0:T(8,128)(2,1)}, u32[]{:S(2)}, u32[]{:S(2)}) collective-permute-start(bf16[128,1408]{1,0:T(8,128)(2,1)} %get-tuple-element.204), channel_id=1, source_target_pairs={{0,2},{1,3},{2,0},{3,1},{4,6},{5,7},{6,4},{7,5},{8,10},{9,11},{10,... | collective-permute-start | bytes 1081352 | tf_op jit(solution)/shard_map/ppermute | solution.py:60
  76.5 27.8 %collective-permute-start.1 = (bf16[128,1408]{1,0:T(8,128)(2,1)}, bf16[128,1408]{1,0:T(8,128)(2,1)}, u32[]{:S(2)}, u32[]{:S(2)}) collective-permute-start(bf16[128,1408]{1,0:T(8,128)(2,1)} %get-tuple-element.204), channel_id=1, source_target_pairs={{0,4},{1,5},{2,6},{3,7},{4,0},{5,1},{6,2},{7,3},{8,12},{9,13},{10,... | collective-permute-start | bytes 1081352 | tf_op jit(solution)/shard_map/ppermute | solution.py:60
  80.0 26.1 %collective-permute-start.2 = (bf16[128,1408]{1,0:T(8,128)(2,1)}, bf16[128,1408]{1,0:T(8,128)(2,1)}, u32[]{:S(2)}, u32[]{:S(2)}) collective-permute-start(bf16[128,1408]{1,0:T(8,128)(2,1)} %get-tuple-element.204), channel_id=1, source_target_pairs={{0,6},{1,7},{2,4},{3,5},{4,2},{5,3},{6,0},{7,1},{8,14},{9,15},{10,... | collective-permute-start | bytes 1081352 | tf_op jit(solution)/shard_map/ppermute | solution.py:60
  83.0 26.1 %collective-permute-start.43 = (bf16[128,1792]{1,0:T(8,128)(2,1)}, bf16[128,1792]{1,0:T(8,128)(2,1)}, u32[]{:S(2)}, u32[]{:S(2)}) collective-permute-start(bf16[128,1792]{1,0:T(8,128)(2,1)} %pad_maximum_fusion.15), channel_id=1, source_target_pairs={{0,1},{1,0},{2,3},{3,2},{4,5},{5,4},{6,7},{7,6},{8,9},{9,8},{10,11... | collective-permute-start | bytes 1376264 | tf_op jit(solution)/shard_map/ppermute | solution.py:60
  83.5 25.6 %collective-permute-start.18 = (bf16[640,128]{0,1:T(8,128)(2,1)}, bf16[640,128]{0,1:T(8,128)(2,1)}, u32[]{:S(2)}, u32[]{:S(2)}) collective-permute-start(bf16[640,128]{0,1:T(8,128)(2,1)} %get-tuple-element.213), channel_id=1, source_target_pairs={{0,1},{1,0},{2,3},{3,2},{4,5},{5,4},{6,7},{7,6},{8,9},{9,8},{10,11... | collective-permute-start | bytes 491528 | tf_op jit(solution)/shard_map/ppermute | solution.py:60
  90.5 20.7 %collective-permute-start.56 = (bf16[2,4,28,640]{3,2,1,0:T(8,128)(2,1)S(1)}, bf16[2,4,28,640]{3,2,1,0:T(8,128)(2,1)S(1)}, u32[]{:S(2)}, u32[]{:S(2)}) collective-permute-start(bf16[2,4,28,640]{3,2,1,0:T(8,128)(2,1)S(1)} %pad_maximum_fusion.24), channel_id=1, source_target_pairs={{0,8},{8,0},{16,24},{24,16},{1,9},{9,1},{17,25},{25,17},{2,10},{10... | collective-permute-start | bytes 860168 | tf_op jit(solution)/shard_map/ppermute | solution.py:60
  111.8 33.9 %collective-permute-start.44 = (bf16[2,4,40,896]{3,2,1,0:T(8,128)(2,1)S(1)}, bf16[2,4,40,896]{3,2,1,0:T(8,128)(2,1)S(1)}, u32[]{:S(2)}, u32[]{:S(2)}) collective-permute-start(bf16[2,4,40,896]{3,2,1,0:T(8,128)(2,1)S(1)} %pad_maximum_fusion.14), channel_id=1, source_target_pairs={{0,8},{8,0},{16,24},{24,16},{1,9},{9,1},{17,25},{25,17},{2,10},{10... | collective-permute-start | bytes 1720328 | tf_op jit(solution)/shard_map/ppermute | solution.py:60
  113.6 18.5 %collective-permute-start.49 = (bf16[2,4,40,896]{3,2,1,0:T(8,128)(2,1)S(1)}, bf16[2,4,40,896]{3,2,1,0:T(8,128)(2,1)S(1)}, u32[]{:S(2)}, u32[]{:S(2)}) collective-permute-start(bf16[2,4,40,896]{3,2,1,0:T(8,128)(2,1)S(1)} %stack.181), channel_id=1, source_target_pairs={{0,16},{8,24},{16,0},{24,8},{1,17},{9,25},{17,1},{25,9},{2,18},{10... | collective-permute-start | bytes 1720328 | tf_op jit(solution)/shard_map/ppermute | solution.py:60
  120.2 19.3 %collective-permute-start.58 = (bf16[28,640]{1,0:T(8,128)(2,1)S(1)}, bf16[28,640]{1,0:T(8,128)(2,1)S(1)}, u32[]{:S(2)}, u32[]{:S(2)}) collective-permute-start(bf16[28,640]{1,0:T(8,128)(2,1)S(1)} %get-tuple-element.228), channel_id=1, source_target_pairs={{0,2},{1,3},{2,0},{3,1},{4,6},{5,7},{6,4},{7,5},{8,10},{9,11},{10,... | collective-permute-start | bytes 107528 | tf_op jit(solution)/shard_map/ppermute | solution.py:60
  143.5 21.7 %collective-permute-start.7 = (bf16[4,128,1280]{1,2,0:T(8,128)(2,1)S(1)}, bf16[4,128,1280]{1,2,0:T(8,128)(2,1)S(1)}, u32[]{:S(2)}, u32[]{:S(2)}) collective-permute-start(bf16[4,128,1280]{1,2,0:T(8,128)(2,1)S(1)} %copy-done.54), channel_id=1, source_target_pairs={{0,1},{1,0},{2,3},{3,2},{4,5},{5,4},{6,7},{7,6},{8,9},{9,8},{10,11... | collective-permute-start | bytes 3932168 | tf_op jit(solution)/shard_map/ppermute | solution.py:60
  154.4 18.7 %collective-permute-start.3 = (bf16[4,128,1408]{2,1,0:T(8,128)(2,1)}, bf16[4,128,1408]{2,1,0:T(8,128)(2,1)}, u32[]{:S(2)}, u32[]{:S(2)}) collective-permute-start(bf16[4,128,1408]{2,1,0:T(8,128)(2,1)} %get-tuple-element.172), channel_id=1, source_target_pairs={{0,1},{1,0},{2,3},{3,2},{4,5},{5,4},{6,7},{7,6},{8,9},{9,8},{10,11... | collective-permute-start | bytes 4325384 | tf_op jit(solution)/shard_map/ppermute | solution.py:60
  231.3 111.2 %collective-permute-start.76 = (bf16[2,224,1280]{2,1,0:T(8,128)(2,1)}, bf16[2,224,1280]{2,1,0:T(8,128)(2,1)}, u32[]{:S(2)}, u32[]{:S(2)}) collective-permute-start(bf16[2,224,1280]{2,1,0:T(8,128)(2,1)} %pad_maximum_fusion.12), channel_id=1, source_target_pairs={{0,16},{8,24},{16,0},{24,8},{1,17},{9,25},{17,1},{25,9},{2,18},{10... | collective-permute-start | bytes 3440648 | tf_op jit(solution)/shard_map/ppermute | solution.py:60
  233.0 41.9 %collective-permute-start.74 = (bf16[2,224,1280]{2,1,0:T(8,128)(2,1)}, bf16[2,224,1280]{2,1,0:T(8,128)(2,1)}, u32[]{:S(2)}, u32[]{:S(2)}) collective-permute-start(bf16[2,224,1280]{2,1,0:T(8,128)(2,1)} %pad_maximum_fusion.11), channel_id=1, source_target_pairs={{0,8},{8,0},{16,24},{24,16},{1,9},{9,1},{17,25},{25,17},{2,10},{10... | collective-permute-start | bytes 3440648 | tf_op jit(solution)/shard_map/ppermute | solution.py:60
  255.8 28.5 %collective-permute-start.70 = (bf16[2,320,896]{2,1,0:T(8,128)(2,1)}, bf16[2,320,896]{2,1,0:T(8,128)(2,1)}, u32[]{:S(2)}, u32[]{:S(2)}) collective-permute-start(bf16[2,320,896]{2,1,0:T(8,128)(2,1)} %pad_maximum_fusion.9), channel_id=1, source_target_pairs={{0,8},{8,0},{16,24},{24,16},{1,9},{9,1},{17,25},{25,17},{2,10},{10... | collective-permute-start | bytes 3440648 | tf_op jit(solution)/shard_map/ppermute | solution.py:60
  258.6 46.7 %collective-permute-start.66 = (bf16[2,320,896]{2,1,0:T(8,128)(2,1)}, bf16[2,320,896]{2,1,0:T(8,128)(2,1)}, u32[]{:S(2)}, u32[]{:S(2)}) collective-permute-start(bf16[2,320,896]{2,1,0:T(8,128)(2,1)} %pad_maximum_fusion.7), channel_id=1, source_target_pairs={{0,8},{8,0},{16,24},{24,16},{1,9},{9,1},{17,25},{25,17},{2,10},{10... | collective-permute-start | bytes 3440648 | tf_op jit(solution)/shard_map/ppermute | solution.py:60
  272.4 35.6 %collective-permute-start.8 = (bf16[4,128,1280]{1,2,0:T(8,128)(2,1)S(1)}, bf16[4,128,1280]{1,2,0:T(8,128)(2,1)S(1)}, u32[]{:S(2)}, u32[]{:S(2)}) collective-permute-start(bf16[4,128,1280]{1,2,0:T(8,128)(2,1)S(1)} %slice.786), channel_id=1, source_target_pairs={{0,1},{1,0},{2,3},{3,2},{4,5},{5,4},{6,7},{7,6},{8,9},{9,8},{10,11... | collective-permute-start | bytes 3932168 | tf_op jit(solution)/shard_map/ppermute | solution.py:60
  274.9 71.4 %collective-permute-start.72 = (bf16[2,320,896]{2,1,0:T(8,128)(2,1)}, bf16[2,320,896]{2,1,0:T(8,128)(2,1)}, u32[]{:S(2)}, u32[]{:S(2)}) collective-permute-start(bf16[2,320,896]{2,1,0:T(8,128)(2,1)} %pad_maximum_fusion.10), channel_id=1, source_target_pairs={{0,16},{8,24},{16,0},{24,8},{1,17},{9,25},{17,1},{25,9},{2,18},{10... | collective-permute-start | bytes 3440648 | tf_op jit(solution)/shard_map/ppermute | solution.py:60
  284.3 24.2 %collective-permute-start.12 = (bf16[4,128,1408]{1,2,0:T(8,128)(2,1)S(1)}, bf16[4,128,1408]{1,2,0:T(8,128)(2,1)S(1)}, u32[]{:S(2)}, u32[]{:S(2)}) collective-permute-start(bf16[4,128,1408]{1,2,0:T(8,128)(2,1)S(1)} %pad_maximum_fusion.3), channel_id=1, source_target_pairs={{0,1},{1,0},{2,3},{3,2},{4,5},{5,4},{6,7},{7,6},{8,9},{9,8},{10,11... | collective-permute-start | bytes 4325384 | tf_op jit(solution)/shard_map/ppermute | solution.py:60
  305.3 37.6 %collective-permute-start.75 = (bf16[1,224,1280]{2,1,0:T(8,128)(2,1)}, bf16[1,224,1280]{2,1,0:T(8,128)(2,1)}, u32[]{:S(2)}, u32[]{:S(2)}) collective-permute-start(bf16[1,224,1280]{2,1,0:T(8,128)(2,1)} %fusion.53), channel_id=1, source_target_pairs={{0,16},{8,24},{16,0},{24,8},{1,17},{9,25},{17,1},{25,9},{2,18},{10... | collective-permute-start | bytes 1720328 | tf_op jit(solution)/shard_map/ppermute | solution.py:60
  308.4 20.0 %collective-permute-start.10 = (bf16[128,1280]{0,1:T(8,128)(2,1)S(1)}, bf16[128,1280]{0,1:T(8,128)(2,1)S(1)}, u32[]{:S(2)}, u32[]{:S(2)}) collective-permute-start(bf16[128,1280]{0,1:T(8,128)(2,1)S(1)} %get-tuple-element.183), channel_id=1, source_target_pairs={{0,4},{1,5},{2,6},{3,7},{4,0},{5,1},{6,2},{7,3},{8,12},{9,13},{10,... | collective-permute-start | bytes 983048 | tf_op jit(solution)/shard_map/ppermute | solution.py:60
  308.5 21.0 %collective-permute-start.11 = (bf16[128,1280]{0,1:T(8,128)(2,1)S(1)}, bf16[128,1280]{0,1:T(8,128)(2,1)S(1)}, u32[]{:S(2)}, u32[]{:S(2)}) collective-permute-start(bf16[128,1280]{0,1:T(8,128)(2,1)S(1)} %get-tuple-element.182), channel_id=1, source_target_pairs={{0,6},{1,7},{2,4},{3,5},{4,2},{5,3},{6,0},{7,1},{8,14},{9,15},{10,... | collective-permute-start | bytes 983048 | tf_op jit(solution)/shard_map/ppermute | solution.py:60
  329.5 45.9 %collective-permute-start.68 = (bf16[2,320,896]{2,1,0:T(8,128)(2,1)}, bf16[2,320,896]{2,1,0:T(8,128)(2,1)}, u32[]{:S(2)}, u32[]{:S(2)}) collective-permute-start(bf16[2,320,896]{2,1,0:T(8,128)(2,1)} %pad_maximum_fusion.8), channel_id=1, source_target_pairs={{0,16},{8,24},{16,0},{24,8},{1,17},{9,25},{17,1},{25,9},{2,18},{10... | collective-permute-start | bytes 3440648 | tf_op jit(solution)/shard_map/ppermute | solution.py:60
  338.0 32.2 %collective-permute-start.71 = (bf16[1,320,896]{2,1,0:T(8,128)(2,1)}, bf16[1,320,896]{2,1,0:T(8,128)(2,1)}, u32[]{:S(2)}, u32[]{:S(2)}) collective-permute-start(bf16[1,320,896]{2,1,0:T(8,128)(2,1)} %fusion.57), channel_id=1, source_target_pairs={{0,16},{8,24},{16,0},{24,8},{1,17},{9,25},{17,1},{25,9},{2,18},{10... | collective-permute-start | bytes 1720328 | tf_op jit(solution)/shard_map/ppermute | solution.py:60
  342.6 38.8 %collective-permute-start.67 = (bf16[1,320,896]{2,1,0:T(8,128)(2,1)}, bf16[1,320,896]{2,1,0:T(8,128)(2,1)S(1)}, u32[]{:S(2)}, u32[]{:S(2)}) collective-permute-start(bf16[1,320,896]{2,1,0:T(8,128)(2,1)} %fusion.61), channel_id=1, source_target_pairs={{0,16},{8,24},{16,0},{24,8},{1,17},{9,25},{17,1},{25,9},{2,18},{10... | collective-permute-start | bytes 1720328 | tf_op jit(solution)/shard_map/ppermute | solution.py:60
  342.9 41.6 %collective-permute-start.13 = (bf16[128,1408]{0,1:T(8,128)(2,1)}, bf16[128,1408]{0,1:T(8,128)(2,1)S(1)}, u32[]{:S(2)}, u32[]{:S(2)}) collective-permute-start(bf16[128,1408]{0,1:T(8,128)(2,1)} %get-tuple-element.168), channel_id=1, source_target_pairs={{0,2},{1,3},{2,0},{3,1},{4,6},{5,7},{6,4},{7,5},{8,10},{9,11},{10,... | collective-permute-start | bytes 1081352 | tf_op jit(solution)/shard_map/ppermute | solution.py:60
  346.4 40.3 %collective-permute-start.14 = (bf16[128,1408]{0,1:T(8,128)(2,1)S(1)}, bf16[128,1408]{0,1:T(8,128)(2,1)S(1)}, u32[]{:S(2)}, u32[]{:S(2)}) collective-permute-start(bf16[128,1408]{0,1:T(8,128)(2,1)S(1)} %copy-done.64), channel_id=1, source_target_pairs={{0,4},{1,5},{2,6},{3,7},{4,0},{5,1},{6,2},{7,3},{8,12},{9,13},{10,... | collective-permute-start | bytes 1081352 | tf_op jit(solution)/shard_map/ppermute | solution.py:60
  370.2 16.4 %collective-permute-start.15 = (bf16[128,1408]{0,1:T(8,128)(2,1)S(1)}, bf16[128,1408]{0,1:T(8,128)(2,1)S(1)}, u32[]{:S(2)}, u32[]{:S(2)}) collective-permute-start(bf16[128,1408]{0,1:T(8,128)(2,1)S(1)} %copy-done.63), channel_id=1, source_target_pairs={{0,6},{1,7},{2,4},{3,5},{4,2},{5,3},{6,0},{7,1},{8,14},{9,15},{10,... | collective-permute-start | bytes 1081352 | tf_op jit(solution)/shard_map/ppermute | solution.py:60
  375.3 47.5 %collective-permute-start.31 = (bf16[640,128]{0,1:T(8,128)(2,1)}, bf16[640,128]{0,1:T(8,128)(2,1)}, u32[]{:S(2)}, u32[]{:S(2)}) collective-permute-start(bf16[640,128]{0,1:T(8,128)(2,1)} %get-tuple-element.206), channel_id=1, source_target_pairs={{0,1},{1,0},{2,3},{3,2},{4,5},{5,4},{6,7},{7,6},{8,9},{9,8},{10,11... | collective-permute-start | bytes 491528 | tf_op jit(solution)/shard_map/ppermute | solution.py:60
  381.4 92.2 %collective-permute-start.16 = (bf16[640,128]{0,1:T(8,128)(2,1)}, bf16[640,128]{0,1:T(8,128)(2,1)}, u32[]{:S(2)}, u32[]{:S(2)}) collective-permute-start(bf16[640,128]{0,1:T(8,128)(2,1)} %get-tuple-element.211), channel_id=1, source_target_pairs={{0,1},{1,0},{2,3},{3,2},{4,5},{5,4},{6,7},{7,6},{8,9},{9,8},{10,11... | collective-permute-start | bytes 491528 | tf_op jit(solution)/shard_map/ppermute | solution.py:60
  384.5 54.5 %collective-permute-start.77 = (bf16[1,224,1280]{2,1,0:T(8,128)(2,1)}, bf16[1,224,1280]{2,1,0:T(8,128)(2,1)}, u32[]{:S(2)}, u32[]{:S(2)}) collective-permute-start(bf16[1,224,1280]{2,1,0:T(8,128)(2,1)} %get-tuple-element.135), channel_id=1, source_target_pairs={{0,8},{8,0},{16,24},{24,16},{1,9},{9,1},{17,25},{25,17},{2,10},{10... | collective-permute-start | bytes 1720328 | tf_op jit(solution)/shard_map/ppermute | solution.py:60
  389.8 34.9 %collective-permute-start.32 = (bf16[128,1280]{0,1:T(8,128)(2,1)}, bf16[128,1280]{0,1:T(8,128)(2,1)}, u32[]{:S(2)}, u32[]{:S(2)}) collective-permute-start(bf16[128,1280]{0,1:T(8,128)(2,1)} %get-tuple-element.128), channel_id=1, source_target_pairs={{0,1},{1,0},{2,3},{3,2},{4,5},{5,4},{6,7},{7,6},{8,9},{9,8},{10,11... | collective-permute-start | bytes 983048 | tf_op jit(solution)/shard_map/ppermute | solution.py:60
  421.3 16.0 %collective-permute-start.73 = (bf16[1,320,896]{2,1,0:T(8,128)(2,1)}, bf16[1,320,896]{2,1,0:T(8,128)(2,1)S(1)}, u32[]{:S(2)}, u32[]{:S(2)}) collective-permute-start(bf16[1,320,896]{2,1,0:T(8,128)(2,1)} %get-tuple-element.141), channel_id=1, source_target_pairs={{0,8},{8,0},{16,24},{24,16},{1,9},{9,1},{17,25},{25,17},{2,10},{10... | collective-permute-start | bytes 1720328 | tf_op jit(solution)/shard_map/ppermute | solution.py:60
  422.9 26.7 %collective-permute-start.69 = (bf16[1,320,896]{2,1,0:T(8,128)(2,1)}, bf16[1,320,896]{2,1,0:T(8,128)(2,1)S(1)}, u32[]{:S(2)}, u32[]{:S(2)}) collective-permute-start(bf16[1,320,896]{2,1,0:T(8,128)(2,1)} %get-tuple-element.147), channel_id=1, source_target_pairs={{0,8},{8,0},{16,24},{24,16},{1,9},{9,1},{17,25},{25,17},{2,10},{10... | collective-permute-start | bytes 1720328 | tf_op jit(solution)/shard_map/ppermute | solution.py:60
  424.7 49.2 %collective-permute-start.17 = (bf16[128,3840]{0,1:T(8,128)(2,1)}, bf16[128,3840]{0,1:T(8,128)(2,1)S(1)}, u32[]{:S(2)}, u32[]{:S(2)}) collective-permute-start(bf16[128,3840]{0,1:T(8,128)(2,1)} %pad_maximum_fusion.13), channel_id=1, source_target_pairs={{0,1},{1,0},{2,3},{3,2},{4,5},{5,4},{6,7},{7,6},{8,9},{9,8},{10,11... | collective-permute-start | bytes 2949128 | tf_op jit(solution)/shard_map/ppermute | solution.py:60
  437.3 20.5 %collective-permute-start.33 = (bf16[2,4,40,640]{3,2,1,0:T(8,128)(2,1)S(1)}, bf16[2,4,40,640]{3,2,1,0:T(8,128)(2,1)S(1)}, u32[]{:S(2)}, u32[]{:S(2)}) collective-permute-start(bf16[2,4,40,640]{3,2,1,0:T(8,128)(2,1)S(1)} %pad_maximum_fusion.18), channel_id=1, source_target_pairs={{0,8},{8,0},{16,24},{24,16},{1,9},{9,1},{17,25},{25,17},{2,10},{10... | collective-permute-start | bytes 1228808 | tf_op jit(solution)/shard_map/ppermute | solution.py:60
  439.0 23.7 %collective-permute-start.38 = (bf16[2,4,40,640]{3,2,1,0:T(8,128)(2,1)S(1)}, bf16[2,4,40,640]{3,2,1,0:T(8,128)(2,1)S(1)}, u32[]{:S(2)}, u32[]{:S(2)}) collective-permute-start(bf16[2,4,40,640]{3,2,1,0:T(8,128)(2,1)S(1)} %stack.180), channel_id=1, source_target_pairs={{0,16},{8,24},{16,0},{24,8},{1,17},{9,25},{17,1},{25,9},{2,18},{10... | collective-permute-start | bytes 1228808 | tf_op jit(solution)/shard_map/ppermute | solution.py:60
  464.6 20.0 %collective-permute-start.35 = (bf16[40,640]{1,0:T(8,128)(2,1)S(1)}, bf16[40,640]{1,0:T(8,128)(2,1)S(1)}, u32[]{:S(2)}, u32[]{:S(2)}) collective-permute-start(bf16[40,640]{1,0:T(8,128)(2,1)S(1)} %get-tuple-element.222), channel_id=1, source_target_pairs={{0,2},{1,3},{2,0},{3,1},{4,6},{5,7},{6,4},{7,5},{8,10},{9,11},{10,... | collective-permute-start | bytes 153608 | tf_op jit(solution)/shard_map/ppermute | solution.py:60
  471.7 15.4 %collective-permute-start.37 = (bf16[40,640]{1,0:T(8,128)(2,1)S(1)}, bf16[40,640]{1,0:T(8,128)(2,1)S(1)}, u32[]{:S(2)}, u32[]{:S(2)}) collective-permute-start(bf16[40,640]{1,0:T(8,128)(2,1)S(1)} %get-tuple-element.224), channel_id=1, source_target_pairs={{0,6},{1,7},{2,4},{3,5},{4,2},{5,3},{6,0},{7,1},{8,14},{9,15},{10,... | collective-permute-start | bytes 153608 | tf_op jit(solution)/shard_map/ppermute | solution.py:60
  480.5 28.5 %collective-permute-start.21 = (bf16[2,4,40,2048]{3,2,1,0:T(8,128)(2,1)S(1)}, bf16[2,4,40,2048]{3,2,1,0:T(8,128)(2,1)S(1)}, u32[]{:S(2)}, u32[]{:S(2)}) collective-permute-start(bf16[2,4,40,2048]{3,2,1,0:T(8,128)(2,1)S(1)} %stack.179), channel_id=1, source_target_pairs={{0,16},{8,24},{16,0},{24,8},{1,17},{9,25},{17,1},{25,9},{2,18},{10... | collective-permute-start | bytes 3932168 | tf_op jit(solution)/shard_map/ppermute | solution.py:60
  482.6 30.3 %collective-permute-start.26 = (bf16[2,4,40,2048]{3,2,1,0:T(8,128)(2,1)S(1)}, bf16[2,4,40,2048]{3,2,1,0:T(8,128)(2,1)S(1)}, u32[]{:S(2)}, u32[]{:S(2)}) collective-permute-start(bf16[2,4,40,2048]{3,2,1,0:T(8,128)(2,1)S(1)} %pad_maximum_fusion.6), channel_id=1, source_target_pairs={{0,8},{8,0},{16,24},{24,16},{1,9},{9,1},{17,25},{25,17},{2,10},{10... | collective-permute-start | bytes 3932168 | tf_op jit(solution)/shard_map/ppermute | solution.py:60
  509.2 15.7 %collective-permute-start.22 = (bf16[1,4,40,2048]{3,2,1,0:T(8,128)(2,1)S(1)}, bf16[1,4,40,2048]{3,2,1,0:T(8,128)(2,1)S(1)}, u32[]{:S(2)}, u32[]{:S(2)}) collective-permute-start(bf16[1,4,40,2048]{3,2,1,0:T(8,128)(2,1)S(1)} %add_convert_fusion.7), channel_id=1, source_target_pairs={{0,8},{8,0},{16,24},{24,16},{1,9},{9,1},{17,25},{25,17},{2,10},{10... | collective-permute-start | bytes 1966088 | tf_op jit(solution)/shard_map/ppermute | solution.py:60
  513.1 16.7 %collective-permute-start.27 = (bf16[1,4,40,2048]{3,2,1,0:T(8,128)(2,1)S(1)}, bf16[1,4,40,2048]{3,2,1,0:T(8,128)(2,1)S(1)}, u32[]{:S(2)}, u32[]{:S(2)}) collective-permute-start(bf16[1,4,40,2048]{3,2,1,0:T(8,128)(2,1)S(1)} %add_convert_fusion.5), channel_id=1, source_target_pairs={{0,16},{8,24},{16,0},{24,8},{1,17},{9,25},{17,1},{25,9},{2,18},{10... | collective-permute-start | bytes 1966088 | tf_op jit(solution)/shard_map/ppermute | solution.py:60
  530.1 23.2 %collective-permute-start.29 = (bf16[40,2048]{1,0:T(8,128)(2,1)S(1)}, bf16[40,2048]{1,0:T(8,128)(2,1)S(1)}, u32[]{:S(2)}, u32[]{:S(2)}) collective-permute-start(bf16[40,2048]{1,0:T(8,128)(2,1)S(1)} %get-tuple-element.194), channel_id=1, source_target_pairs={{0,4},{1,5},{2,6},{3,7},{4,0},{5,1},{6,2},{7,3},{8,12},{9,13},{10,... | collective-permute-start | bytes 491528 | tf_op jit(solution)/shard_map/ppermute | solution.py:60
  534.7 18.7 %collective-permute-start.30 = (bf16[40,2048]{1,0:T(8,128)(2,1)S(1)}, bf16[40,2048]{1,0:T(8,128)(2,1)S(1)}, u32[]{:S(2)}, u32[]{:S(2)}) collective-permute-start(bf16[40,2048]{1,0:T(8,128)(2,1)S(1)} %get-tuple-element.195), channel_id=1, source_target_pairs={{0,6},{1,7},{2,4},{3,5},{4,2},{5,3},{6,0},{7,1},{8,14},{9,15},{10,... | collective-permute-start | bytes 491528 | tf_op jit(solution)/shard_map/ppermute | solution.py:60
  (135 other events, 962.8 us)
